TPU v7x, 256 devices: a whole 4x4x8 slice. The times are simulated.
256 devices in a mesh: tm: 32 (over z, y), feat: 8 (over x, core).
Axes of the slice: x: 4, y: 4, z: 8, core: 2. Of those that a mesh axis runs over, the one named last changes fastest.
Arguments:
- tile_data: bfloat16 [2048, 32, 128, 128], P('tm', 'feat'), may hold values from -1 to 1
- tile_ids: int32 [2048, 32], P('tm', 'feat'), may hold values from 0 to 31, as said below
- owner_perm: int32 [2048], P('tm'), may hold values from 0 to 2047, as said below
- events: int32 [2048, 128], P('tm'), may hold values 0 or 1
- groups: int32 [2048, 128], P('tm'), may hold values from 0 to 127, as said below
- coefficients: bfloat16 [32768], P('feat'), may hold values from -4 to 4
Outputs:
- gradient: float32 [32768], P('feat')
- newton_step: float32 [32768], P('feat')
Inputs may be any that keep to these rules, and one draw needn't show every extreme that they name: `tile_ids`: in each feature shard's 4 columns a row block names 4 different local feature blocks. `owner_perm`: A permutation of row blocks; each patient shard of 64 row blocks sends exactly 2 of them to each time shard. `groups`: group numbers start at 0 in every row block and never fall within it; a tied group never spans two row blocks.
All inputs are finite; a program needn't handle non-finite values. No bound on the sum of `events` on one device may be relied on, other than what follows from the above.
Results may differ from a plain program's by a relative error of at most 0.00035.
The roundings to bfloat16 on the way count: a program that leaves them out, or rounds other values in their place, can miss the bound.
Values may be sent and summed in bfloat16 or wider, within the bound.
A program may use at most 128 MiB of HBM per device.

v0:
```python
import jax
import jax.numpy as jnp
from jax import lax
from jax.sharding import PartitionSpec as P

ridge_weight = 1.0


def entering(part, axis, combine, identity, reverse):
    count = lax.axis_size(axis)
    place = lax.axis_index(axis)
    ahead = count - 1 - place if reverse else place
    gathered = jax.tree.map(lambda a: lax.all_gather(a, axis), part)
    state = jax.tree.map(lambda a, e: jnp.zeros_like(a) + jnp.asarray(e, a.dtype), part, identity)

    def one(turn, state):
        source = count - 1 - turn if reverse else turn
        return combine(
            state, jax.tree.map(lambda a: lax.dynamic_index_in_dim(a, source, 0, False), gathered)
        )

    return lax.fori_loop(0, ahead, one, state)


def add_pair(earlier, later):
    return (earlier[0] + later[0], earlier[1] + later[1])


def add_one(earlier, later):
    return earlier + later


def solve_blocks(grad_blocks, hess_blocks):
    tile_width = hess_blocks.shape[1]
    system = hess_blocks + ridge_weight * jnp.eye(tile_width, dtype=jnp.float32)[None]
    factor = jnp.linalg.cholesky(system)
    return jax.scipy.linalg.cho_solve((factor, True), grad_blocks[:, :, None])[:, :, 0]


def local(tile_data, tile_ids, owner_perm, events, groups, coefficients):
    row_count = tile_data.shape[0]
    tile_width = tile_data.shape[2]
    shard_count = lax.axis_size("tm")
    per_pair = row_count // shard_count
    local_blocks = coefficients.shape[0] // tile_width
    coef_blocks = coefficients.reshape(local_blocks, tile_width)
    block_range = jnp.arange(local_blocks, dtype=jnp.int32)
    target = owner_perm // row_count
    arrival_slot = owner_perm % row_count
    sorting = jnp.argsort(target, stable=True)
    outgoing = (
        tile_data[sorting].reshape(
            shard_count, per_pair, tile_data.shape[1], tile_width, tile_width
        ),
        tile_ids[sorting].reshape(shard_count, per_pair, tile_ids.shape[1]),
        events[sorting].reshape(shard_count, per_pair, tile_width),
        arrival_slot[sorting].reshape(shard_count, per_pair),
    )
    received = (
        lax.all_to_all(outgoing[0], "tm", split_axis=0, concat_axis=0, tiled=True),
        lax.all_to_all(outgoing[1], "tm", split_axis=0, concat_axis=0, tiled=True),
        lax.all_to_all(outgoing[2], "tm", split_axis=0, concat_axis=0, tiled=True),
        lax.all_to_all(outgoing[3], "tm", split_axis=0, concat_axis=0, tiled=True),
    )
    arrival = received[3].reshape(row_count)
    restore_order = jnp.argsort(arrival)
    time_tiles = received[0].reshape(row_count, tile_data.shape[1], tile_width, tile_width)[
        restore_order
    ]
    time_ids = received[1].reshape(row_count, tile_ids.shape[1])[restore_order]
    time_events = received[2].reshape(row_count, tile_width)[restore_order]
    onehot = (time_ids[:, :, None] == block_range[None, None, :]).astype(jnp.bfloat16)
    picked = jnp.einsum(
        "nsj,jt->nst", onehot, coef_blocks, preferred_element_type=jnp.float32
    ).astype(jnp.bfloat16)
    time_eta = lax.psum(
        jnp.einsum("nspt,nst->np", time_tiles, picked, preferred_element_type=jnp.float32), "feat"
    )
    event_flag = time_events.astype(jnp.float32)
    risk_score = jnp.exp(time_eta)
    later_mask = (groups[:, None, :] >= groups[:, :, None]).astype(jnp.float32)
    later_in = jnp.einsum("bik,bk->bi", later_mask, risk_score, precision=lax.Precision.HIGHEST)
    block_tot = jnp.sum(risk_score, axis=1)
    device_tot = jnp.sum(block_tot)
    after_device = entering(device_tot, "tm", add_one, jnp.zeros((), jnp.float32), True)
    after_blocks = jnp.concatenate(
        [jnp.cumsum(block_tot[::-1])[::-1][1:], jnp.zeros((1,), jnp.float32)]
    )
    risk_total = after_device + after_blocks[:, None] + later_in
    hazard_one = event_flag / risk_total
    hazard_two = hazard_one / risk_total
    earlier_one = jnp.einsum("bki,bk->bi", later_mask, hazard_one, precision=lax.Precision.HIGHEST)
    earlier_two = jnp.einsum("bki,bk->bi", later_mask, hazard_two, precision=lax.Precision.HIGHEST)
    tot_one = jnp.sum(hazard_one, axis=1)
    tot_two = jnp.sum(hazard_two, axis=1)
    zero_scalar = jnp.zeros((), jnp.float32)
    before_dev = entering(
        (jnp.sum(tot_one), jnp.sum(tot_two)), "tm", add_pair, (zero_scalar, zero_scalar), False
    )
    before_one = jnp.concatenate([jnp.zeros((1,), jnp.float32), jnp.cumsum(tot_one)[:-1]])
    before_two = jnp.concatenate([jnp.zeros((1,), jnp.float32), jnp.cumsum(tot_two)[:-1]])
    cum_one = before_dev[0] + before_one[:, None] + earlier_one
    cum_two = before_dev[1] + before_two[:, None] + earlier_two
    residual = event_flag - risk_score * cum_one
    weight = risk_score * cum_one - risk_score * risk_score * cum_two
    residual, weight = (residual, weight)
    resid_round = residual.astype(jnp.bfloat16)
    weighted = (time_tiles * weight[:, None, :, None]).astype(jnp.bfloat16)
    grad_slots = jnp.einsum(
        "nspa,np->nsa", time_tiles, resid_round, preferred_element_type=jnp.float32
    )
    hess_slots = jnp.einsum(
        "nspa,nspb->nsab", weighted, time_tiles, preferred_element_type=jnp.float32
    )
    flat_ids = time_ids.reshape(-1)
    grad_local = (
        jnp.zeros((local_blocks, tile_width), jnp.float32)
        .at[flat_ids]
        .add(grad_slots.reshape(-1, tile_width))
    )
    hess_local = (
        jnp.zeros((local_blocks, tile_width, tile_width), jnp.float32)
        .at[flat_ids]
        .add(hess_slots.reshape(-1, tile_width, tile_width))
    )
    grad_local, hess_local = (grad_local, hess_local)
    grad_part, hess_part = (
        lax.psum_scatter(grad_local, "tm", scatter_dimension=0, tiled=True),
        lax.psum_scatter(hess_local, "tm", scatter_dimension=0, tiled=True),
    )
    step_part = solve_blocks(grad_part, hess_part)
    gradient, newton_step = (
        lax.all_gather(grad_part, "tm", axis=0, tiled=True),
        lax.all_gather(step_part, "tm", axis=0, tiled=True),
    )
    return (gradient.reshape(-1), newton_step.reshape(-1))


def solution(mesh):
    return jax.shard_map(
        local,
        mesh=mesh,
        in_specs=(
            P("tm", "feat", None, None),
            P("tm", "feat"),
            P("tm"),
            P("tm", None),
            P("tm", None),
            P("feat"),
        ),
        out_specs=(P("feat"), P("feat")),
        check_vma=False,
    )
```

profile of v0, /device:TPU:2, one launch (start us, length us, event | category | flops | bytes accessed | tf_op | source)
XLA Modules:
  0.0 893.4 jit_solution(6770830898521049463)
XLA Ops:
  11.4 11.5 %all-to-all-start.1 = ((s32[32,1,2]{2,1,0:T(1,128)}), s32[32,1,2]{2,1,0:T(1,128)S(1)}, u32[]{:S(2)}, u32[]{:S(2)}) async-start(s32[32,1,2]{2,1,0:T(1,128)} %bitcast.5), calls=%async_computation.1 | async-start | bytes 32768 | tf_op jit(solution)/shard_map/all_to_all | solution.py:63
  24.8 7.7 all-to-all-done.1
  32.5 3.8 all-to-all-start
  37.6 8.6 all-to-all-done
  46.2 3.9 all-to-all-start.3
  50.0 8.9 gather_fusion.3
  59.8 9.2 %all-to-all-start.2 = ((bf16[32,2,4,128,128]{4,3,2,1,0:T(8,128)(2,1)}), bf16[32,2,4,128,128]{4,3,2,1,0:T(8,128)(2,1)}, u32[]{:S(2)}, u32[]{:S(2)}) async-start(bf16[32,2,4,128,128]{4,3,2,1,0:T(8,128)(2,1)} %bitcast.89), calls=%async_computation.2 | async-start | bytes 16777216 | tf_op jit(solution)/shard_map/all_to_all | solution.py:60
  74.7 173.6 %all-to-all-done.2 = bf16[32,2,4,128,128]{4,3,2,1,0:T(8,128)(2,1)} async-done(((bf16[32,2,4,128,128]{4,3,2,1,0:T(8,128)(2,1)}), bf16[32,2,4,128,128]{4,3,2,1,0:T(8,128)(2,1)}, u32[]{:S(2)}, u32[]{:S(2)}) %all-to-all-start.2) | async-done | bytes 8388640 | tf_op jit(solution)/shard_map/all_to_all | solution.py:60
  248.3 8.9 gather_fusion.4
  257.2 5.6 fusion.15
  262.8 20.7 %psum.7 = f32[64,128]{1,0:T(8,128)S(1)} all-reduce(f32[64,128]{1,0:T(8,128)S(1)} %bitcast.96), channel_id=1, replica_groups=mesh['tm'=32,'feat'=8] {'feat'}, use_global_device_ids=true, to_apply=%region_2.3 | all-reduce | flops 8192 | bytes 65536 | tf_op jit(solution)/shard_map/psum | solution.py:76
  285.5 75.4 %all-reduce = f32[32]{0:T(128)S(1)} all-reduce(f32[32]{0:T(128)S(1)} %dynamic-update-slice.3), channel_id=1, replica_groups=mesh['tm'=32,'feat'=8] {'tm'}, use_global_device_ids=true, to_apply=%add | all-reduce | flops 32 | bytes 256
  361.0 39.0 %while.24 = (s32[]{:T(128)}, f32[]{:T(128)}, s32[]{:T(128)}, f32[32]{0:T(128)S(1)}, s32[]{:T(128)}, /*index=5*/s32[]{:T(128)}, s32[]{:T(128)}, s32[]{:T(128)}) while((s32[]{:T(128)}, f32[]{:T(128)}, s32[]{:T(128)}, f32[32]{0:T(128)S(1)}, s32[]{:T(128)}, /*index=5*/s32[]{:T(128)}, s32[]{:T(128)}, s32[]{:T(128)}) %tuple.56), condition=%wide.region_5.6_spmd, body=%wide.region_4.5_spmd.sunk | while | flops 7 | bytes 163 | solution.py:22
  400.5 4.0 fusion.6
  413.8 69.6 %all-reduce.4 = (f32[32]{0:T(128)S(1)}, f32[32]{0:T(128)S(1)}) all-reduce(f32[32]{0:T(128)S(1)} %dynamic-update-slice.4, f32[32]{0:T(128)S(1)} %dynamic-update-slice.5), channel_id=1, replica_groups=mesh['tm'=32,'feat'=8] {'tm'}, use_global_device_ids=true, to_apply=%add.1 | all-reduce | flops 64 | bytes 512
  484.5 13.4 %fusion = f32[64,4,128,128]{3,2,1,0:T(8,128)} fusion(bf16[64,4,128,128]{3,2,1,0:T(8,128)(2,1)} %gather_fusion.4, f32[64,128]{1,0:T(8,128)S(1)} %get-tuple-element.129), kind=kOutput, calls=%fused_computation.10 | convolution fusion | flops 1086324736 | bytes 25198592 | tf_op jit(solution)/shard_map/nspa,nspb->nsab/dot_general | solution.py:112
  498.1 33.2 %scatter_fusion = f32[32,128,128]{2,1,0:T(8,128)S(1)} fusion(f32[32,128,128]{2,1,0:T(8,128)S(1)} %broadcast_in_dim.14, s32[256]{0:T(256)S(1)} %bitcast.102, f32[256,128,128]{2,1,0:T(8,128)} %bitcast.88), kind=kCustom, calls=%fused_computation.8 | custom fusion | flops 4194304 | bytes 50332672 | tf_op jit(solution)/shard_map/scatter-add | solution.py:124
  532.7 4.6 fusion.20
  538.7 217.3 %all-reduce.3 = f32[32,128]{1,0:T(8,128)S(1)} all-reduce(f32[32,128]{1,0:T(8,128)S(1)} %scatter_custom_fusion), channel_id=3, replica_groups=mesh['tm'=32,'feat'=8] {'tm'}, use_global_device_ids=true, to_apply=%region_15.16.clone | all-reduce | flops 4096 | bytes 32768
  756.7 34.4 %all-gather.1 = f32[32,1,128]{2,1,0:T(1,128)S(1)} all-gather(f32[1,1,128]{2,1,0:T(1,128)S(1)} %fusion.30), channel_id=1, replica_groups=mesh['tm'=32,'feat'=8] {'tm'}, dimensions={0}, use_global_device_ids=true | all-gather | bytes 16896 | tf_op jit(solution)/shard_map/all_gather | solution.py:133
  791.1 31.2 %reduce-scatter.2.cloned.1.call-done = f32[1,128,128]{2,1,0:T(8,128)} async-done(((f32[32,128,128]{2,1,0:T(8,128)}), f32[1,128,128]{2,1,0:T(8,128)}) %reduce-scatter.2.cloned.1.call-update) | async-done | bytes 65552 | tf_op jit(solution)/shard_map/reduce_scatter | solution.py:129
  824.2 11.7 %custom-call.11 = f32[1,128,128]{2,1,0:T(8,128)S(1)} custom-call(f32[1,128,128]{2,1,0:T(8,128)S(1)} %fusion.19), custom_call_target="Cholesky" | custom-call | tf_op jit(solution)/shard_map/jit(cholesky)/cholesky | solution.py:36
  837.2 9.8 %custom-call.12 = f32[1,128,128]{1,2,0:T(8,128)S(1)} custom-call(f32[1,128,128]{2,1,0:T(8,128)S(1)} %select_select_fusion), custom_call_target="InvertDiagBlocksLowerTriangular" | custom-call | tf_op jit(solution)/shard_map/jit(_cho_solve)/triangular_solve | solution.py:37
  848.1 37.2 %all-gather.2 = f32[32,1,128]{2,1,0:T(1,128)S(1)} all-gather(f32[1,1,128]{2,1,0:T(1,128)S(1)} %convolution_bitcast_fusion), channel_id=2, replica_groups=mesh['tm'=32,'feat'=8] {'tm'}, dimensions={0}, use_global_device_ids=true | all-gather | bytes 16896 | tf_op jit(solution)/shard_map/all_gather | solution.py:134
  (106 shorter events, 54.0 us)
Async XLA Ops:
  7.2 29.2 %copy-start = (s32[64,128]{1,0:T(8,128)S(1)}, s32[64,128]{1,0:T(8,128)}, u32[]{:S(2)}) copy-start(s32[64,128]{1,0:T(8,128)} %param.13) | copy-start | bytes 98308
  11.4 21.2 %all-to-all-start.1 = ((s32[32,1,2]{2,1,0:T(1,128)}), s32[32,1,2]{2,1,0:T(1,128)S(1)}, u32[]{:S(2)}, u32[]{:S(2)}) async-start(s32[32,1,2]{2,1,0:T(1,128)} %bitcast.5), calls=%async_computation.1 | async-start | bytes 32768 | tf_op jit(solution)/shard_map/all_to_all | solution.py:63
  32.5 13.6 %all-to-all-start = ((s32[32,2,4]{2,1,0:T(2,128)}), s32[32,2,4]{2,1,0:T(2,128)S(1)}, u32[]{:S(2)}, u32[]{:S(2)}) async-start(s32[32,2,4]{2,1,0:T(2,128)} %bitcast.3), calls=%async_computation | async-start | bytes 65536 | tf_op jit(solution)/shard_map/all_to_all | solution.py:61
  46.2 13.6 %all-to-all-start.3 = ((s32[32,2,128]{2,1,0:T(2,128)}), s32[32,2,128]{2,1,0:T(2,128)S(1)}, u32[]{:S(2)}, u32[]{:S(2)}) async-start(s32[32,2,128]{2,1,0:T(2,128)} %bitcast.9), calls=%async_computation.3 | async-start | bytes 65536 | tf_op jit(solution)/shard_map/all_to_all | solution.py:62
  59.8 9.3 %copy-start.3 = (u32[256]{0:T(256)S(1)}, u32[256]{0:T(256)}, u32[]{:S(2)}) copy-start(u32[256]{0:T(256)} %constant.148) | copy-start | bytes 3076
  59.8 14.1 %copy-start.2 = (bf16[4096]{0:T(1024)(128)(2,1)S(1)}, bf16[4096]{0:T(1024)(128)(2,1)}, u32[]{:S(2)}) copy-start(bf16[4096]{0:T(1024)(128)(2,1)} %param.15) | copy-start | bytes 24580
  59.8 188.5 %all-to-all-start.2 = ((bf16[32,2,4,128,128]{4,3,2,1,0:T(8,128)(2,1)}), bf16[32,2,4,128,128]{4,3,2,1,0:T(8,128)(2,1)}, u32[]{:S(2)}, u32[]{:S(2)}) async-start(bf16[32,2,4,128,128]{4,3,2,1,0:T(8,128)(2,1)} %bitcast.89), calls=%async_computation.2 | async-start | bytes 16777216 | tf_op jit(solution)/shard_map/all_to_all | solution.py:60
  69.0 753.3 %reduce-scatter.2.cloned.1.call-start = ((), (), s32[]{:S(2)}) async-start(), calls=%async_computation.5 | async-start | bytes 2162688 | tf_op jit(solution)/shard_map/reduce_scatter | solution.py:129
  257.2 143.3 %copy-start.4 = (s32[64,128]{1,0:T(8,128)S(1)}, s32[64,128]{1,0:T(8,128)}, u32[]{:S(2)}) copy-start(s32[64,128]{1,0:T(8,128)} %param.14) | copy-start | bytes 98308
  531.3 1.4 copy-start.1
Sparse Core Ops, SparseCore 0:
  532.8 289.4 reduce-scatter.1
where the time goes:
time: 896 us; the launch traced here: 893 us
  blocking collectives  455 us (51%)
  waiting for transfers between devices  222 us (25%)
  other arithmetic  66.5 us (7%)
  local copies, waits for them, and re-layouts  51.8 us (6%)
  matrix products  34.7 us (4%)
  starting transfers between devices  28.4 us (3%)
  loops' own time  21 us (2%)
  between operations  14.3 us (2%)
    unnamed x3, blocking collectives  362 us
    all_to_all x1, waiting for transfers between devices, local(): lax.all_to_all(outgoing[0], 'tm', split_axis=0, concat_axis=0, tiled=True)  174 us
    all_gather x1, blocking collectives, local(): lax.all_gather(step_part, 'tm', axis=0, tiled=True)  37.2 us
    all_gather x1, blocking collectives, local(): lax.all_gather(grad_part, 'tm', axis=0, tiled=True)  34.4 us
    scatter-add x1, other arithmetic, local(): hess_local = jnp.zeros((local_blocks, tile_width, tile_width), jnp.float3...  33.2 us
    reduce_scatter x1, waiting for transfers between devices, local(): lax.psum_scatter(hess_local, 'tm', scatter_dimension=0, tiled=True)  31.2 us
    another operation x2, loops' own time, entering(): return lax.fori_loop(0, ahead, one, state)  21 us
    psum x1, blocking collectives, local(): lax.psum(jnp.einsum('nspt,nst->np', time_tiles, picked, preferred_element...  20.7 us
  transfers between devices with their start and end apart: 5, of which 5 were waited for; matrix products, arithmetic and copies ran while one was open for 3% of the time, Pallas kernels for 0%

commit v1 on v0

--- a/solution.py
+++ b/solution.py
@@ -73,8 +73,12 @@
     picked = jnp.einsum(
         "nsj,jt->nst", onehot, coef_blocks, preferred_element_type=jnp.float32
     ).astype(jnp.bfloat16)
-    time_eta = lax.psum(
-        jnp.einsum("nspt,nst->np", time_tiles, picked, preferred_element_type=jnp.float32), "feat"
+    time_eta = jnp.sum(
+        lax.all_gather(
+            jnp.einsum("nspt,nst->np", time_tiles, picked, preferred_element_type=jnp.float32),
+            "feat",
+        ),
+        axis=0,
     )
     event_flag = time_events.astype(jnp.float32)
     risk_score = jnp.exp(time_eta)

time: 896 us -> 887 us (0.990)
  blocking collectives: 455 us -> 446 us
    psum x1 -> x0, blocking collectives: 20.7 us -> none  [local(): lax.psum(jnp.einsum('nspt,nst->np', time_tiles, picked, preferred_element...]
    all_gather x0 -> x1, blocking collectives: none -> 12.9 us  [local(): lax.all_gather(jnp.einsum('nspt,nst->np', time_tiles, picked, preferred_e...]
where the time goes in v1:
time: 887 us; the launch traced here: 884 us
  blocking collectives  446 us (50%)
  waiting for transfers between devices  221 us (25%)
  other arithmetic  66.6 us (8%)
  local copies, waits for them, and re-layouts  51.8 us (6%)
  matrix products  34.7 us (4%)
  starting transfers between devices  28.4 us (3%)
  loops' own time  21 us (2%)
  between operations  14.3 us (2%)
    unnamed x3, blocking collectives  361 us
    all_to_all x1, waiting for transfers between devices, local(): lax.all_to_all(outgoing[0], 'tm', split_axis=0, concat_axis=0, tiled=True)  174 us
    all_gather x1, blocking collectives, local(): lax.all_gather(step_part, 'tm', axis=0, tiled=True)  37.2 us
    all_gather x1, blocking collectives, local(): lax.all_gather(grad_part, 'tm', axis=0, tiled=True)  34.4 us
    scatter-add x1, other arithmetic, local(): hess_local = jnp.zeros((local_blocks, tile_width, tile_width), jnp.float3...  33.2 us
    reduce_scatter x1, waiting for transfers between devices, local(): lax.psum_scatter(hess_local, 'tm', scatter_dimension=0, tiled=True)  30.3 us
    another operation x2, loops' own time, entering(): return lax.fori_loop(0, ahead, one, state)  21 us
    dynamic_slice x31, local copies, waits for them, and re-layouts, one(): lax.dynamic_index_in_dim(a, source, 0, False)  18.2 us
  transfers between devices with their start and end apart: 5, of which 5 were waited for; matrix products, arithmetic and copies ran while one was open for 3% of the time, Pallas kernels for 0%

profile of v1, /device:TPU:2, one launch (start us, length us, event | category | flops | bytes accessed | tf_op | source)
XLA Modules:
  0.0 883.5 jit_solution(9461065375173440845)
XLA Ops:
  11.4 11.5 %all-to-all-start.1 = ((s32[32,1,2]{2,1,0:T(1,128)}), s32[32,1,2]{2,1,0:T(1,128)S(1)}, u32[]{:S(2)}, u32[]{:S(2)}) async-start(s32[32,1,2]{2,1,0:T(1,128)} %bitcast.5), calls=%async_computation.1 | async-start | bytes 32768 | tf_op jit(solution)/shard_map/all_to_all | solution.py:63
  24.8 7.7 all-to-all-done.1
  32.5 3.8 all-to-all-start
  37.6 8.6 all-to-all-done
  46.2 3.9 all-to-all-start.3
  50.0 8.9 %gather_fusion.3 = bf16[64,4,128,128]{3,2,1,0:T(8,128)(2,1)} fusion(bf16[64,4,128,128]{3,2,1,0:T(8,128)(2,1)} %param.10, s32[1024]{0:T(1024)S(1)} %pad_clamp_fusion.1), kind=kCustom, calls=%fused_computation.3 | custom fusion | bytes 16777472 | tf_op jit(solution)/shard_map/gather | solution.py:52
  59.8 9.2 %all-to-all-start.2 = ((bf16[32,2,4,128,128]{4,3,2,1,0:T(8,128)(2,1)}), bf16[32,2,4,128,128]{4,3,2,1,0:T(8,128)(2,1)}, u32[]{:S(2)}, u32[]{:S(2)}) async-start(bf16[32,2,4,128,128]{4,3,2,1,0:T(8,128)(2,1)} %bitcast.90), calls=%async_computation.2 | async-start | bytes 16777216 | tf_op jit(solution)/shard_map/all_to_all | solution.py:60
  74.7 173.6 %all-to-all-done.2 = bf16[32,2,4,128,128]{4,3,2,1,0:T(8,128)(2,1)} async-done(((bf16[32,2,4,128,128]{4,3,2,1,0:T(8,128)(2,1)}), bf16[32,2,4,128,128]{4,3,2,1,0:T(8,128)(2,1)}, u32[]{:S(2)}, u32[]{:S(2)}) %all-to-all-start.2) | async-done | bytes 8388640 | tf_op jit(solution)/shard_map/all_to_all | solution.py:60
  248.3 8.9 %gather_fusion.4 = bf16[64,4,128,128]{3,2,1,0:T(8,128)(2,1)} fusion(bf16[64,4,128,128]{3,2,1,0:T(8,128)(2,1)} %bitcast.8, s32[1024]{0:T(1024)S(1)} %pad_clamp_fusion), kind=kCustom, calls=%fused_computation.4 | custom fusion | bytes 16777472 | tf_op jit(solution)/shard_map/gather | solution.py:67
  257.2 5.6 fusion.15
  262.8 12.9 %all-gather = f32[512,128]{1,0:T(8,128)S(1)} all-gather(f32[64,128]{1,0:T(8,128)S(1)} %bitcast.97), channel_id=2, replica_groups=mesh['tm'=32,'feat'=8] {'feat'}, dimensions={0}, use_global_device_ids=true | all-gather | bytes 294912 | tf_op jit(solution)/shard_map/all_gather | solution.py:77
  277.8 74.3 %all-reduce = f32[32]{0:T(128)S(1)} all-reduce(f32[32]{0:T(128)S(1)} %dynamic-update-slice.3), channel_id=1, replica_groups=mesh['tm'=32,'feat'=8] {'tm'}, use_global_device_ids=true, to_apply=%add | all-reduce | flops 32 | bytes 256
  352.1 39.0 %while.24 = (s32[]{:T(128)}, f32[]{:T(128)}, s32[]{:T(128)}, f32[32]{0:T(128)S(1)}, s32[]{:T(128)}, /*index=5*/s32[]{:T(128)}, s32[]{:T(128)}, s32[]{:T(128)}) while((s32[]{:T(128)}, f32[]{:T(128)}, s32[]{:T(128)}, f32[32]{0:T(128)S(1)}, s32[]{:T(128)}, /*index=5*/s32[]{:T(128)}, s32[]{:T(128)}, s32[]{:T(128)}) %tuple.56), condition=%wide.region_5.6_spmd, body=%wide.region_4.5_spmd.sunk | while | flops 7 | bytes 163 | solution.py:22
  391.6 4.0 fusion.6
  404.9 69.6 %all-reduce.4 = (f32[32]{0:T(128)S(1)}, f32[32]{0:T(128)S(1)}) all-reduce(f32[32]{0:T(128)S(1)} %dynamic-update-slice.4, f32[32]{0:T(128)S(1)} %dynamic-update-slice.5), channel_id=1, replica_groups=mesh['tm'=32,'feat'=8] {'tm'}, use_global_device_ids=true, to_apply=%add.1 | all-reduce | flops 64 | bytes 512
  475.5 13.4 %fusion = f32[64,4,128,128]{3,2,1,0:T(8,128)} fusion(bf16[64,4,128,128]{3,2,1,0:T(8,128)(2,1)} %gather_fusion.4, f32[64,128]{1,0:T(8,128)S(1)} %get-tuple-element.129), kind=kOutput, calls=%fused_computation.10 | convolution fusion | flops 1086324736 | bytes 25198592 | tf_op jit(solution)/shard_map/nspa,nspb->nsab/dot_general | solution.py:116
  489.2 33.2 %scatter_fusion = f32[32,128,128]{2,1,0:T(8,128)S(1)} fusion(f32[32,128,128]{2,1,0:T(8,128)S(1)} %broadcast_in_dim.14, s32[256]{0:T(256)S(1)} %bitcast.104, f32[256,128,128]{2,1,0:T(8,128)} %bitcast.89), kind=kCustom, calls=%fused_computation.8 | custom fusion | flops 4194304 | bytes 50332672 | tf_op jit(solution)/shard_map/scatter-add | solution.py:128
  523.8 4.6 fusion.20
  529.8 217.3 %all-reduce.3 = f32[32,128]{1,0:T(8,128)S(1)} all-reduce(f32[32,128]{1,0:T(8,128)S(1)} %scatter_custom_fusion), channel_id=4, replica_groups=mesh['tm'=32,'feat'=8] {'tm'}, use_global_device_ids=true, to_apply=%region_15.16.clone | all-reduce | flops 4096 | bytes 32768
  747.8 34.4 %all-gather.2 = f32[32,1,128]{2,1,0:T(1,128)S(1)} all-gather(f32[1,1,128]{2,1,0:T(1,128)S(1)} %fusion.30), channel_id=1, replica_groups=mesh['tm'=32,'feat'=8] {'tm'}, dimensions={0}, use_global_device_ids=true | all-gather | bytes 16896 | tf_op jit(solution)/shard_map/all_gather | solution.py:137
  782.3 30.3 %reduce-scatter.2.cloned.1.call-done = f32[1,128,128]{2,1,0:T(8,128)} async-done(((f32[32,128,128]{2,1,0:T(8,128)}), f32[1,128,128]{2,1,0:T(8,128)}) %reduce-scatter.2.cloned.1.call-update) | async-done | bytes 65552 | tf_op jit(solution)/shard_map/reduce_scatter | solution.py:133
  814.4 11.7 %custom-call.11 = f32[1,128,128]{2,1,0:T(8,128)S(1)} custom-call(f32[1,128,128]{2,1,0:T(8,128)S(1)} %fusion.19), custom_call_target="Cholesky" | custom-call | tf_op jit(solution)/shard_map/jit(cholesky)/cholesky | solution.py:36
  827.4 9.8 %custom-call.12 = f32[1,128,128]{1,2,0:T(8,128)S(1)} custom-call(f32[1,128,128]{2,1,0:T(8,128)S(1)} %select_select_fusion), custom_call_target="InvertDiagBlocksLowerTriangular" | custom-call | tf_op jit(solution)/shard_map/jit(_cho_solve)/triangular_solve | solution.py:37
  838.3 37.2 %all-gather.3 = f32[32,1,128]{2,1,0:T(1,128)S(1)} all-gather(f32[1,1,128]{2,1,0:T(1,128)S(1)} %convolution_bitcast_fusion), channel_id=3, replica_groups=mesh['tm'=32,'feat'=8] {'tm'}, dimensions={0}, use_global_device_ids=true | all-gather | bytes 16896 | tf_op jit(solution)/shard_map/all_gather | solution.py:138
  (107 shorter events, 54.0 us)
Async XLA Ops:
  7.2 29.2 %copy-start = (s32[64,128]{1,0:T(8,128)S(1)}, s32[64,128]{1,0:T(8,128)}, u32[]{:S(2)}) copy-start(s32[64,128]{1,0:T(8,128)} %param.13) | copy-start | bytes 98308
  11.4 21.2 %all-to-all-start.1 = ((s32[32,1,2]{2,1,0:T(1,128)}), s32[32,1,2]{2,1,0:T(1,128)S(1)}, u32[]{:S(2)}, u32[]{:S(2)}) async-start(s32[32,1,2]{2,1,0:T(1,128)} %bitcast.5), calls=%async_computation.1 | async-start | bytes 32768 | tf_op jit(solution)/shard_map/all_to_all | solution.py:63
  32.5 13.6 %all-to-all-start = ((s32[32,2,4]{2,1,0:T(2,128)}), s32[32,2,4]{2,1,0:T(2,128)S(1)}, u32[]{:S(2)}, u32[]{:S(2)}) async-start(s32[32,2,4]{2,1,0:T(2,128)} %bitcast.3), calls=%async_computation | async-start | bytes 65536 | tf_op jit(solution)/shard_map/all_to_all | solution.py:61
  46.2 13.6 %all-to-all-start.3 = ((s32[32,2,128]{2,1,0:T(2,128)}), s32[32,2,128]{2,1,0:T(2,128)S(1)}, u32[]{:S(2)}, u32[]{:S(2)}) async-start(s32[32,2,128]{2,1,0:T(2,128)} %bitcast.9), calls=%async_computation.3 | async-start | bytes 65536 | tf_op jit(solution)/shard_map/all_to_all | solution.py:62
  59.8 9.3 %copy-start.3 = (u32[256]{0:T(256)S(1)}, u32[256]{0:T(256)}, u32[]{:S(2)}) copy-start(u32[256]{0:T(256)} %constant.148) | copy-start | bytes 3076
  59.8 14.1 %copy-start.2 = (bf16[4096]{0:T(1024)(128)(2,1)S(1)}, bf16[4096]{0:T(1024)(128)(2,1)}, u32[]{:S(2)}) copy-start(bf16[4096]{0:T(1024)(128)(2,1)} %param.15) | copy-start | bytes 24580
  59.8 188.5 %all-to-all-start.2 = ((bf16[32,2,4,128,128]{4,3,2,1,0:T(8,128)(2,1)}), bf16[32,2,4,128,128]{4,3,2,1,0:T(8,128)(2,1)}, u32[]{:S(2)}, u32[]{:S(2)}) async-start(bf16[32,2,4,128,128]{4,3,2,1,0:T(8,128)(2,1)} %bitcast.90), calls=%async_computation.2 | async-start | bytes 16777216 | tf_op jit(solution)/shard_map/all_to_all | solution.py:60
  69.0 743.6 %reduce-scatter.2.cloned.1.call-start = ((), (), s32[]{:S(2)}) async-start(), calls=%async_computation.5 | async-start | bytes 2162688 | tf_op jit(solution)/shard_map/reduce_scatter | solution.py:133
  257.2 134.3 %copy-start.4 = (s32[64,128]{1,0:T(8,128)S(1)}, s32[64,128]{1,0:T(8,128)}, u32[]{:S(2)}) copy-start(s32[64,128]{1,0:T(8,128)} %param.14) | copy-start | bytes 98308
  522.4 1.4 copy-start.1
Sparse Core Ops, SparseCore 0:
  523.9 288.6 reduce-scatter.1
